TPU v7x, 512 devices: a whole 4x4x16 slice. The times are simulated.
512 devices in a mesh: cuts: 32 (over z, x_lo), blk: 16 (over x_hi, y, core).
Axes of the slice: x: 4 (x_hi: 2, x_lo: 2; x = x_hi * 2 + x_lo), y: 4, z: 16, core: 2. Of those that a mesh axis runs over, the one named last changes fastest.
Arguments:
- steps: bfloat16 [512, 2, 512, 512], P(('cuts', 'blk')), as said below
Outputs:
- sidebands: float32 [32, 2, 512, 512], P(None, None, 'blk', 'cuts')
Inputs may be any that keep to these rules, and one draw needn't show every extreme that they name: `steps`: sqrt(512) times every entry lies between -1 and 1.
All inputs are finite; a program needn't handle non-finite values.
Results may differ from a plain program's by a relative error of at most 0.035.
Values may be sent and summed in bfloat16 or wider, within the bound.
A program may use at most 64 MiB of HBM per device.

v0:
```python
import math
import jax
import jax.numpy as jnp
from jax import lax
from jax.sharding import PartitionSpec as P


def from_partner(block, axis, distance):
    count = lax.axis_size(axis)
    route = []
    for low in range(count):
        high = low | 1 << distance
        if high != low and high < count:
            route += [(low, high), (high, low)]
    return lax.ppermute(block, axis, route)


def passed_along(x, axis, by):
    devices = lax.axis_size(axis)
    return lax.ppermute(x, axis, [(i, (i + by) % devices) for i in range(devices)])


def complex_product(left_factor, right_factor):
    real_real = jnp.dot(left_factor[0], right_factor[0], preferred_element_type=jnp.float32)
    imag_imag = jnp.dot(left_factor[1], right_factor[1], preferred_element_type=jnp.float32)
    real_imag = jnp.dot(left_factor[0], right_factor[1], preferred_element_type=jnp.float32)
    imag_real = jnp.dot(left_factor[1], right_factor[0], preferred_element_type=jnp.float32)
    return jnp.stack([real_real - imag_imag, real_imag + imag_real])


def complex_wide(left_factor, right_factor):
    hp = lax.Precision.HIGHEST
    real_real = jnp.dot(left_factor[0], right_factor[0], precision=hp)
    imag_imag = jnp.dot(left_factor[1], right_factor[1], precision=hp)
    real_imag = jnp.dot(left_factor[0], right_factor[1], precision=hp)
    imag_real = jnp.dot(left_factor[1], right_factor[0], precision=hp)
    return jnp.stack([real_real - imag_imag, real_imag + imag_real])


def group_product(left_factor, right_factor):
    if left_factor.dtype == jnp.bfloat16:
        return complex_product(left_factor, right_factor)
    return complex_wide(left_factor, right_factor)


def per_device(steps):
    current = steps[0]
    order = current.shape[-1]
    blk_count = lax.axis_size("blk")
    block_rows = order // blk_count
    tree_depth = blk_count.bit_length() - 1
    blk_index = lax.axis_index("blk")
    first_partner = from_partner(current, "blk", 0)
    for section in range(tree_depth):
        if section == 0:
            partner = first_partner
        else:
            partner = from_partner(current, "blk", section)
        is_upper = blk_index >> section & 1 == 1
        upper_factor = jnp.where(is_upper, current, partner)
        lower_factor = jnp.where(is_upper, partner, current)
        current = group_product(upper_factor, lower_factor)
    current = current.astype(jnp.bfloat16)
    row_block = lax.dynamic_slice_in_dim(current, blk_index * block_rows, block_rows, 1)
    cuts_count = lax.axis_size("cuts")
    loop_depth = cuts_count.bit_length() - 1
    for section in range(loop_depth):
        distance = 1 << section
        ahead = passed_along(row_block, "cuts", -distance)

        def add_rows(running, incoming, offset, ahead=ahead):
            return complex_product(ahead, incoming)

        empty_sum = jnp.zeros(row_block.shape, jnp.float32)
        running = add_rows(
            empty_sum, lax.all_gather(row_block, "blk", axis=1, tiled=True), jnp.int32(0)
        )
        row_block = running.astype(jnp.bfloat16)
    received = lax.all_to_all(row_block[None], "cuts", split_axis=3, concat_axis=0, tiled=True)
    slice_count = received.shape[0]
    freq_index = jnp.arange(slice_count, dtype=jnp.int32)
    phase_angle = (
        2.0
        * math.pi
        / slice_count
        * (freq_index[:, None] * freq_index[None, :] % slice_count).astype(jnp.float32)
    )
    cosine_table = jnp.cos(phase_angle)
    sine_table = jnp.sin(phase_angle)
    flattened = received.astype(jnp.float32).reshape(slice_count, 2, -1)
    hp = lax.Precision.HIGHEST
    real_part = jnp.dot(cosine_table, flattened[:, 0], precision=hp) + jnp.dot(
        sine_table, flattened[:, 1], precision=hp
    )
    imag_part = jnp.dot(cosine_table, flattened[:, 1], precision=hp) - jnp.dot(
        sine_table, flattened[:, 0], precision=hp
    )
    norm_factor = math.sqrt(order / slice_count)
    result = jnp.stack([real_part, imag_part], axis=1) * norm_factor
    return result.reshape(received.shape)


def solution(mesh):
    in_specs = (P(("cuts", "blk"), None, None, None),)
    out_specs = P(None, None, "blk", "cuts")
    return jax.shard_map(
        per_device, mesh=mesh, in_specs=in_specs, out_specs=out_specs, check_vma=False
    )
```

profile of v0, /device:TPU:2, one launch (start us, length us, event | category | flops | bytes accessed | tf_op | source)
XLA Modules:
  0.0 564.4 jit_solution(16650119582925848394)
XLA Ops:
  6.5 1.9 collective-permute-start
  8.5 2.8 collective-permute-done
  11.3 1.4 broadcast_select_fusion.1
  14.4 1.5 pad_maximum_fusion
  15.9 3.5 collective-permute-start.1
  19.4 46.4 %collective-permute-done.1 = f32[2,512,512]{2,1,0:T(8,128)} collective-permute-done((f32[2,512,512]{2,1,0:T(8,128)}, f32[2,512,512]{2,1,0:T(8,128)}, u32[]{:S(2)}, u32[]{:S(2)}) %collective-permute-start.1) | collective-permute-done | bytes 2097184 | tf_op jit(solution)/shard_map/ppermute | solution.py:15
  65.8 2.3 broadcast_select_fusion.3
  68.1 1.8 fusion.31
  70.0 1.8 fusion.30
  71.8 1.8 fusion.3
  73.7 1.8 fusion.2
  75.6 1.5 pad_maximum_fusion.1
  77.1 5.3 collective-permute-start.2
  82.3 45.3 %collective-permute-done.2 = f32[2,512,512]{2,1,0:T(8,128)} collective-permute-done((f32[2,512,512]{2,1,0:T(8,128)}, f32[2,512,512]{2,1,0:T(8,128)}, u32[]{:S(2)}, u32[]{:S(2)}) %collective-permute-start.2) | collective-permute-done | bytes 2097184 | tf_op jit(solution)/shard_map/ppermute | solution.py:15
  127.6 2.3 broadcast_select_fusion.5
  129.9 1.8 fusion.33
  131.8 1.8 fusion.32
  133.7 1.8 fusion.1
  135.5 1.8 fusion
  137.4 1.5 pad_maximum_fusion.2
  138.9 4.2 collective-permute-start.3
  143.1 45.4 %collective-permute-done.3 = f32[2,512,512]{2,1,0:T(8,128)} collective-permute-done((f32[2,512,512]{2,1,0:T(8,128)}, f32[2,512,512]{2,1,0:T(8,128)}, u32[]{:S(2)}, u32[]{:S(2)}) %collective-permute-start.3) | collective-permute-done | bytes 2097184 | tf_op jit(solution)/shard_map/ppermute | solution.py:15
  188.5 2.3 broadcast_select_fusion.6
  190.8 1.9 fusion.34
  192.7 1.9 fusion.35
  194.6 1.9 fusion.8
  196.4 1.9 fusion.9
  199.1 7.8 %collective-permute-start.4 = (bf16[2,32,512]{2,1,0:T(8,128)(2,1)}, bf16[2,32,512]{2,1,0:T(8,128)(2,1)S(1)}, u32[]{:S(2)}, u32[]{:S(2)}) collective-permute-start(bf16[2,32,512]{2,1,0:T(8,128)(2,1)} %fusion.50), channel_id=1, source_target_pairs={{0,496},{16,0},{32,16},{48,32},{64,48},{80,64},{96,80},{112,96},{1... | collective-permute-start | bytes 196616 | tf_op jit(solution)/shard_map/ppermute | solution.py:20
  206.9 2.2 collective-permute-done.4
  209.1 53.8 %all-gather.6.cloned.1.call-done = bf16[2,512,512]{2,1,0:T(8,128)(2,1)} async-done(((bf16[2,32,512]{2,1,0:T(8,128)(2,1)}), bf16[2,512,512]{2,1,0:T(8,128)(2,1)}) %all-gather.6.cloned.1.call-update) | async-done | bytes 1048592 | tf_op jit(solution)/shard_map/all_gather | solution.py:76
  262.9 1.2 fusion.39
  264.1 1.2 fusion.38
  265.4 1.2 fusion.29
  266.6 1.2 fusion.28
  268.6 6.0 %collective-permute-start.5 = (bf16[2,32,512]{2,1,0:T(8,128)(2,1)}, bf16[2,32,512]{2,1,0:T(8,128)(2,1)S(1)}, u32[]{:S(2)}, u32[]{:S(2)}) collective-permute-start(bf16[2,32,512]{2,1,0:T(8,128)(2,1)} %pad_maximum_fusion.3), channel_id=1, source_target_pairs={{0,480},{16,496},{32,0},{48,16},{64,32},{80,48},{96,64},{112,80},{... | collective-permute-start | bytes 196616 | tf_op jit(solution)/shard_map/ppermute | solution.py:20
  274.5 2.2 collective-permute-done.5
  276.7 51.0 %all-gather.8.cloned.1.call-done = bf16[2,512,512]{2,1,0:T(8,128)(2,1)} async-done(((bf16[2,32,512]{2,1,0:T(8,128)(2,1)}), bf16[2,512,512]{2,1,0:T(8,128)(2,1)}) %all-gather.8.cloned.1.call-update) | async-done | bytes 1048592 | tf_op jit(solution)/shard_map/all_gather | solution.py:76
  327.7 1.2 fusion.41
  328.9 1.2 fusion.40
  330.1 1.2 fusion.27
  331.4 1.2 fusion.26
  333.3 6.8 %collective-permute-start.6 = (bf16[2,32,512]{2,1,0:T(8,128)(2,1)}, bf16[2,32,512]{2,1,0:T(8,128)(2,1)S(1)}, u32[]{:S(2)}, u32[]{:S(2)}) collective-permute-start(bf16[2,32,512]{2,1,0:T(8,128)(2,1)} %pad_maximum_fusion.4), channel_id=1, source_target_pairs={{0,448},{16,464},{32,480},{48,496},{64,0},{80,16},{96,32},{112,48}... | collective-permute-start | bytes 196616 | tf_op jit(solution)/shard_map/ppermute | solution.py:20
  340.1 3.5 collective-permute-done.6
  343.6 48.8 %all-gather.10.cloned.1.call-done = bf16[2,512,512]{2,1,0:T(8,128)(2,1)} async-done(((bf16[2,32,512]{2,1,0:T(8,128)(2,1)}), bf16[2,512,512]{2,1,0:T(8,128)(2,1)}) %all-gather.10.cloned.1.call-update) | async-done | bytes 1048592 | tf_op jit(solution)/shard_map/all_gather | solution.py:76
  392.5 1.2 fusion.43
  393.7 1.2 fusion.42
  394.9 1.2 fusion.25
  396.2 1.2 fusion.24
  398.1 8.4 %collective-permute-start.7 = (bf16[2,32,512]{2,1,0:T(8,128)(2,1)}, bf16[2,32,512]{2,1,0:T(8,128)(2,1)S(1)}, u32[]{:S(2)}, u32[]{:S(2)}) collective-permute-start(bf16[2,32,512]{2,1,0:T(8,128)(2,1)} %pad_maximum_fusion.5), channel_id=1, source_target_pairs={{0,384},{16,400},{32,416},{48,432},{64,448},{80,464},{96,480},{112... | collective-permute-start | bytes 196616 | tf_op jit(solution)/shard_map/ppermute | solution.py:20
  406.5 6.3 %collective-permute-done.7 = bf16[2,32,512]{2,1,0:T(8,128)(2,1)S(1)} collective-permute-done((bf16[2,32,512]{2,1,0:T(8,128)(2,1)}, bf16[2,32,512]{2,1,0:T(8,128)(2,1)S(1)}, u32[]{:S(2)}, u32[]{:S(2)}) %collective-permute-start.7) | collective-permute-done | bytes 65568 | tf_op jit(solution)/shard_map/ppermute | solution.py:20
  412.8 44.4 %all-gather.12.cloned.1.call-done = bf16[2,512,512]{2,1,0:T(8,128)(2,1)} async-done(((bf16[2,32,512]{2,1,0:T(8,128)(2,1)}), bf16[2,512,512]{2,1,0:T(8,128)(2,1)}) %all-gather.12.cloned.1.call-update) | async-done | bytes 1048592 | tf_op jit(solution)/shard_map/all_gather | solution.py:76
  457.2 1.2 fusion.45
  458.5 1.2 fusion.44
  459.7 1.2 fusion.23
  460.9 1.2 fusion.22
  462.9 12.8 %collective-permute-start.8 = (bf16[2,32,512]{2,1,0:T(8,128)(2,1)}, bf16[2,32,512]{2,1,0:T(8,128)(2,1)S(1)}, u32[]{:S(2)}, u32[]{:S(2)}) collective-permute-start(bf16[2,32,512]{2,1,0:T(8,128)(2,1)} %pad_maximum_fusion.6), channel_id=1, source_target_pairs={{0,256},{16,272},{32,288},{48,304},{64,320},{80,336},{96,352},{112... | collective-permute-start | bytes 196616 | tf_op jit(solution)/shard_map/ppermute | solution.py:20
  475.7 3.0 collective-permute-done.8
  478.7 43.3 %all-gather.14.cloned.1.call-done = bf16[2,512,512]{2,1,0:T(8,128)(2,1)} async-done(((bf16[2,32,512]{2,1,0:T(8,128)(2,1)}), bf16[2,512,512]{2,1,0:T(8,128)(2,1)}) %all-gather.14.cloned.1.call-update) | async-done | bytes 1048592 | tf_op jit(solution)/shard_map/all_gather | solution.py:76
  522.0 1.2 fusion.47
  523.3 1.2 fusion.46
  524.5 1.2 fusion.21
  525.7 1.2 fusion.20
  527.4 27.2 %all_to_all.15 = bf16[32,2,512]{2,1,0:T(2,128)(2,1)S(1)} all-to-all(bf16[32,2,512]{2,1,0:T(2,128)(2,1)S(1)} %reshape.43), channel_id=1, replica_groups=mesh['cuts'=32,'blk'=16] {'cuts'}, dimensions={0} | all-to-all | bytes 131072 | tf_op jit(solution)/shard_map/all_to_all | solution.py:79
  556.6 1.3 copy.18
  (32 shorter events, 7.6 us)
Async XLA Ops:
  6.5 256.4 %all-gather.6.cloned.1.call-start = ((), (), s32[]{:S(2)}) async-start(), calls=%async_computation.1 | async-start | bytes 1114112 | tf_op jit(solution)/shard_map/all_gather | solution.py:76
  6.5 4.8 collective-permute-start
  15.9 49.9 %collective-permute-start.1 = (f32[2,512,512]{2,1,0:T(8,128)}, f32[2,512,512]{2,1,0:T(8,128)}, u32[]{:S(2)}, u32[]{:S(2)}) collective-permute-start(f32[2,512,512]{2,1,0:T(8,128)} %pad_maximum_fusion), channel_id=1, source_target_pairs={{0,2},{2,0},{1,3},{3,1},{4,6},{6,4},{5,7},{7,5},{8,10},{10,8},{9,1... | collective-permute-start | bytes 6291464 | tf_op jit(solution)/shard_map/ppermute | solution.py:15
  77.1 50.5 %collective-permute-start.2 = (f32[2,512,512]{2,1,0:T(8,128)}, f32[2,512,512]{2,1,0:T(8,128)}, u32[]{:S(2)}, u32[]{:S(2)}) collective-permute-start(f32[2,512,512]{2,1,0:T(8,128)} %pad_maximum_fusion.1), channel_id=1, source_target_pairs={{0,4},{4,0},{1,5},{5,1},{2,6},{6,2},{3,7},{7,3},{8,12},{12,8},{9,1... | collective-permute-start | bytes 6291464 | tf_op jit(solution)/shard_map/ppermute | solution.py:15
  138.9 49.6 %collective-permute-start.3 = (f32[2,512,512]{2,1,0:T(8,128)}, f32[2,512,512]{2,1,0:T(8,128)}, u32[]{:S(2)}, u32[]{:S(2)}) collective-permute-start(f32[2,512,512]{2,1,0:T(8,128)} %pad_maximum_fusion.2), channel_id=1, source_target_pairs={{0,8},{8,0},{1,9},{9,1},{2,10},{10,2},{3,11},{11,3},{4,12},{12,4},... | collective-permute-start | bytes 6291464 | tf_op jit(solution)/shard_map/ppermute | solution.py:15
  199.0 128.7 %all-gather.8.cloned.1.call-start = ((), (), s32[]{:S(2)}) async-start(), calls=%async_computation.2 | async-start | bytes 1114112 | tf_op jit(solution)/shard_map/all_gather | solution.py:76
  199.1 10.0 %collective-permute-start.4 = (bf16[2,32,512]{2,1,0:T(8,128)(2,1)}, bf16[2,32,512]{2,1,0:T(8,128)(2,1)S(1)}, u32[]{:S(2)}, u32[]{:S(2)}) collective-permute-start(bf16[2,32,512]{2,1,0:T(8,128)(2,1)} %fusion.50), channel_id=1, source_target_pairs={{0,496},{16,0},{32,16},{48,32},{64,48},{80,64},{96,80},{112,96},{1... | collective-permute-start | bytes 196616 | tf_op jit(solution)/shard_map/ppermute | solution.py:20
  268.5 123.9 %all-gather.10.cloned.1.call-start = ((), (), s32[]{:S(2)}) async-start(), calls=%async_computation.3 | async-start | bytes 1114112 | tf_op jit(solution)/shard_map/all_gather | solution.py:76
  268.6 8.2 %collective-permute-start.5 = (bf16[2,32,512]{2,1,0:T(8,128)(2,1)}, bf16[2,32,512]{2,1,0:T(8,128)(2,1)S(1)}, u32[]{:S(2)}, u32[]{:S(2)}) collective-permute-start(bf16[2,32,512]{2,1,0:T(8,128)(2,1)} %pad_maximum_fusion.3), channel_id=1, source_target_pairs={{0,480},{16,496},{32,0},{48,16},{64,32},{80,48},{96,64},{112,80},{... | collective-permute-start | bytes 196616 | tf_op jit(solution)/shard_map/ppermute | solution.py:20
  333.3 123.9 %all-gather.12.cloned.1.call-start = ((), (), s32[]{:S(2)}) async-start(), calls=%async_computation.4 | async-start | bytes 1114112 | tf_op jit(solution)/shard_map/all_gather | solution.py:76
  333.3 10.3 %collective-permute-start.6 = (bf16[2,32,512]{2,1,0:T(8,128)(2,1)}, bf16[2,32,512]{2,1,0:T(8,128)(2,1)S(1)}, u32[]{:S(2)}, u32[]{:S(2)}) collective-permute-start(bf16[2,32,512]{2,1,0:T(8,128)(2,1)} %pad_maximum_fusion.4), channel_id=1, source_target_pairs={{0,448},{16,464},{32,480},{48,496},{64,0},{80,16},{96,32},{112,48}... | collective-permute-start | bytes 196616 | tf_op jit(solution)/shard_map/ppermute | solution.py:20
  398.1 123.9 %all-gather.14.cloned.1.call-start = ((), (), s32[]{:S(2)}) async-start(), calls=%async_computation.5 | async-start | bytes 1114112 | tf_op jit(solution)/shard_map/all_gather | solution.py:76
  398.1 14.7 %collective-permute-start.7 = (bf16[2,32,512]{2,1,0:T(8,128)(2,1)}, bf16[2,32,512]{2,1,0:T(8,128)(2,1)S(1)}, u32[]{:S(2)}, u32[]{:S(2)}) collective-permute-start(bf16[2,32,512]{2,1,0:T(8,128)(2,1)} %pad_maximum_fusion.5), channel_id=1, source_target_pairs={{0,384},{16,400},{32,416},{48,432},{64,448},{80,464},{96,480},{112... | collective-permute-start | bytes 196616 | tf_op jit(solution)/shard_map/ppermute | solution.py:20
  462.9 15.8 %collective-permute-start.8 = (bf16[2,32,512]{2,1,0:T(8,128)(2,1)}, bf16[2,32,512]{2,1,0:T(8,128)(2,1)S(1)}, u32[]{:S(2)}, u32[]{:S(2)}) collective-permute-start(bf16[2,32,512]{2,1,0:T(8,128)(2,1)} %pad_maximum_fusion.6), channel_id=1, source_target_pairs={{0,256},{16,272},{32,288},{48,304},{64,320},{80,336},{96,352},{112... | collective-permute-start | bytes 196616 | tf_op jit(solution)/shard_map/ppermute | solution.py:20
Sparse Core Ops, SparseCore 0:
  199.1 63.7 all-gather.5
  268.6 58.9 all-gather.7
  333.4 58.9 all-gather.9
  398.2 58.9 all-gather.11
  463.0 58.9 all-gather.13
where the time goes:
time: 566 us; the launch traced here: 564 us
  waiting for transfers between devices  398 us (70%)
  starting transfers between devices  56.8 us (10%)
  matrix products  49.7 us (9%)
  blocking collectives  27.2 us (5%)
  other arithmetic  16.2 us (3%)
  between operations  13.5 us (2%)
    all_gather x5, waiting for transfers between devices, per_device(): lax.all_gather(row_block, 'blk', axis=1, tiled=True)  241 us
    ppermute x4, waiting for transfers between devices, from_partner(): return lax.ppermute(block, axis, route)  140 us
    ppermute x5, starting transfers between devices, passed_along(): lax.ppermute(x, axis, [(i, (i + by) % devices) for i in range(devices)])  41.7 us
    all_to_all x1, blocking collectives, per_device(): lax.all_to_all(row_block[None], 'cuts', split_axis=3, concat_axis=0, tile...  27.2 us
    ppermute x5, waiting for transfers between devices, passed_along(): lax.ppermute(x, axis, [(i, (i + by) % devices) for i in range(devices)])  17.3 us
    ppermute x4, starting transfers between devices, from_partner(): return lax.ppermute(block, axis, route)  14.9 us
  transfers between devices with their start and end apart: 14, of which 14 were waited for; matrix products, arithmetic and copies ran while one was open for 0% of the time, Pallas kernels for 0%

commit v1 on v0

--- a/solution.py
+++ b/solution.py
@@ -3,6 +3,7 @@
 import jax.numpy as jnp
 from jax import lax
 from jax.sharding import PartitionSpec as P
+from jax.lax import all_to_all, psum
 
 
 def from_partner(block, axis, distance):
@@ -73,7 +74,17 @@
 
         empty_sum = jnp.zeros(row_block.shape, jnp.float32)
         running = add_rows(
-            empty_sum, lax.all_gather(row_block, "blk", axis=1, tiled=True), jnp.int32(0)
+            empty_sum,
+            jnp.concatenate(
+                all_to_all(
+                    jnp.stack([row_block] * psum(1, axis_name="blk"), axis=0),
+                    axis_name="blk",
+                    split_axis=0,
+                    concat_axis=0,
+                ),
+                axis=1,
+            ),
+            jnp.int32(0),
         )
         row_block = running.astype(jnp.bfloat16)
     received = lax.all_to_all(row_block[None], "cuts", split_axis=3, concat_axis=0, tiled=True)

time: 566 us -> 350 us (0.62)
  the two profiles are of different devices: /device:TPU:2 before, /device:TPU:6 now
where the time goes in v1:
time: 350 us; the launch traced here: 349 us
  waiting for transfers between devices  168 us (48%)
  starting transfers between devices  101 us (29%)
  blocking collectives  29.2 us (8%)
  matrix products  28.9 us (8%)
  other arithmetic  13 us (4%)
  local copies, waits for them, and re-layouts  8.62 us (2%)
    ppermute x4, waiting for transfers between devices, from_partner(): return lax.ppermute(block, axis, route)  141 us
    ppermute x5, starting transfers between devices, passed_along(): lax.ppermute(x, axis, [(i, (i + by) % devices) for i in range(devices)])  51.9 us
    all_to_all x5, starting transfers between devices, per_device(): all_to_all(jnp.stack([row_block] * psum(1, axis_name='blk'), axis=0), axi...  34.7 us
    all_to_all x1, blocking collectives, per_device(): lax.all_to_all(row_block[None], 'cuts', split_axis=3, concat_axis=0, tile...  29.2 us
    all_to_all x5, waiting for transfers between devices, per_device(): all_to_all(jnp.stack([row_block] * psum(1, axis_name='blk'), axis=0), axi...  24.2 us
    ppermute x4, starting transfers between devices, from_partner(): return lax.ppermute(block, axis, route)  14.2 us
  transfers between devices with their start and end apart: 14, of which 10 were waited for; matrix products, arithmetic and copies ran while one was open for 0% of the time, Pallas kernels for 0%

profile of v1, /device:TPU:6, one launch (start us, length us, event | category | flops | bytes accessed | tf_op | source)
XLA Modules:
  0.0 348.7 jit_solution(1214684627302529441)
XLA Ops:
  0.0 1.9 collective-permute-start
  1.9 2.8 collective-permute-done
  4.8 1.4 broadcast_select_fusion.1
  6.1 0.4 fusion.37
  6.6 0.4 fusion.36
  7.0 0.4 fusion.5
  7.4 0.4 fusion.4
  7.9 1.5 pad_maximum_fusion
  9.4 3.5 collective-permute-start.1
  12.9 46.4 %collective-permute-done.1 = f32[2,512,512]{2,1,0:T(8,128)} collective-permute-done((f32[2,512,512]{2,1,0:T(8,128)}, f32[2,512,512]{2,1,0:T(8,128)}, u32[]{:S(2)}, u32[]{:S(2)}) %collective-permute-start.1) | collective-permute-done | bytes 2097184 | tf_op jit(solution)/shard_map/ppermute | solution.py:16
  59.3 2.3 broadcast_select_fusion.3
  61.6 1.8 fusion.31
  63.4 1.8 fusion.30
  65.3 1.9 fusion.3
  67.2 1.8 fusion.2
  69.0 1.5 pad_maximum_fusion.1
  70.5 5.3 %collective-permute-start.2 = (f32[2,512,512]{2,1,0:T(8,128)}, f32[2,512,512]{2,1,0:T(8,128)}, u32[]{:S(2)}, u32[]{:S(2)}) collective-permute-start(f32[2,512,512]{2,1,0:T(8,128)} %pad_maximum_fusion.1), channel_id=1, source_target_pairs={{0,4},{4,0},{1,5},{5,1},{2,6},{6,2},{3,7},{7,3},{8,12},{12,8},{9,1... | collective-permute-start | bytes 6291464 | tf_op jit(solution)/shard_map/ppermute | solution.py:16
  75.8 45.3 %collective-permute-done.2 = f32[2,512,512]{2,1,0:T(8,128)} collective-permute-done((f32[2,512,512]{2,1,0:T(8,128)}, f32[2,512,512]{2,1,0:T(8,128)}, u32[]{:S(2)}, u32[]{:S(2)}) %collective-permute-start.2) | collective-permute-done | bytes 2097184 | tf_op jit(solution)/shard_map/ppermute | solution.py:16
  121.1 2.3 broadcast_select_fusion.5
  123.4 1.9 fusion.33
  125.3 1.8 fusion.32
  127.1 1.8 fusion.1
  129.0 1.8 fusion
  130.8 1.5 pad_maximum_fusion.2
  132.3 3.5 %collective-permute-start.3 = (f32[2,512,512]{2,1,0:T(8,128)}, f32[2,512,512]{2,1,0:T(8,128)}, u32[]{:S(2)}, u32[]{:S(2)}) collective-permute-start(f32[2,512,512]{2,1,0:T(8,128)} %pad_maximum_fusion.2), channel_id=1, source_target_pairs={{0,8},{8,0},{1,9},{9,1},{2,10},{10,2},{3,11},{11,3},{4,12},{12,4},... | collective-permute-start | bytes 6291464 | tf_op jit(solution)/shard_map/ppermute | solution.py:16
  135.9 46.1 %collective-permute-done.3 = f32[2,512,512]{2,1,0:T(8,128)} collective-permute-done((f32[2,512,512]{2,1,0:T(8,128)}, f32[2,512,512]{2,1,0:T(8,128)}, u32[]{:S(2)}, u32[]{:S(2)}) %collective-permute-start.3) | collective-permute-done | bytes 2097184 | tf_op jit(solution)/shard_map/ppermute | solution.py:16
  181.9 2.3 broadcast_select_fusion.6
  184.3 1.9 fusion.34
  186.1 1.9 fusion.35
  188.0 1.9 fusion.8
  189.9 1.9 fusion.9
  191.8 1.1 stack.97
  192.9 7.5 %all-to-all-start = ((bf16[16,2,32,512]{3,2,1,0:T(8,128)(2,1)}), bf16[16,2,32,512]{3,2,1,0:T(8,128)(2,1)S(1)}, u32[]{:S(2)}, u32[]{:S(2)}) async-start(bf16[16,2,32,512]{3,2,1,0:T(8,128)(2,1)} %stack.97), calls=%async_computation | async-start | bytes 2097152 | tf_op jit(solution)/shard_map/all_to_all | solution.py:79
  200.4 4.6 %collective-permute-start.4 = (bf16[2,32,512]{2,1,0:T(8,128)(2,1)S(1)}, bf16[2,32,512]{2,1,0:T(8,128)(2,1)S(1)}, u32[]{:S(2)}, u32[]{:S(2)}) collective-permute-start(bf16[2,32,512]{2,1,0:T(8,128)(2,1)S(1)} %fusion.40), channel_id=1, source_target_pairs={{0,496},{16,0},{32,16},{48,32},{64,48},{80,64},{96,80},{112,96},{1... | collective-permute-start | bytes 196616 | tf_op jit(solution)/shard_map/ppermute | solution.py:21
  205.1 10.9 %all-to-all-done = bf16[16,2,32,512]{3,2,1,0:T(8,128)(2,1)S(1)} async-done(((bf16[16,2,32,512]{3,2,1,0:T(8,128)(2,1)}), bf16[16,2,32,512]{3,2,1,0:T(8,128)(2,1)S(1)}, u32[]{:S(2)}, u32[]{:S(2)}) %all-to-all-start) | async-done | bytes 1048608 | tf_op jit(solution)/shard_map/all_to_all | solution.py:79
  216.7 0.2 fusion.28
  216.9 1.1 stack.101
  218.0 6.5 %all-to-all-start.1 = ((bf16[16,2,32,512]{3,2,1,0:T(8,128)(2,1)}), bf16[16,2,32,512]{3,2,1,0:T(8,128)(2,1)S(1)}, u32[]{:S(2)}, u32[]{:S(2)}) async-start(bf16[16,2,32,512]{3,2,1,0:T(8,128)(2,1)} %stack.101), calls=%async_computation.1 | async-start | bytes 2097152 | tf_op jit(solution)/shard_map/all_to_all | solution.py:79
  224.5 11.4 %collective-permute-start.5 = (bf16[2,32,512]{2,1,0:T(8,128)(2,1)S(1)}, bf16[2,32,512]{2,1,0:T(8,128)(2,1)S(1)}, u32[]{:S(2)}, u32[]{:S(2)}) collective-permute-start(bf16[2,32,512]{2,1,0:T(8,128)(2,1)S(1)} %pad_maximum_fusion.3), channel_id=1, source_target_pairs={{0,480},{16,496},{32,0},{48,16},{64,32},{80,48},{96,64},{112,80},{... | collective-permute-start | bytes 196616 | tf_op jit(solution)/shard_map/ppermute | solution.py:21
  235.9 3.8 %all-to-all-done.1 = bf16[16,2,32,512]{3,2,1,0:T(8,128)(2,1)S(1)} async-done(((bf16[16,2,32,512]{3,2,1,0:T(8,128)(2,1)}), bf16[16,2,32,512]{3,2,1,0:T(8,128)(2,1)S(1)}, u32[]{:S(2)}, u32[]{:S(2)}) %all-to-all-start.1) | async-done | bytes 1048608 | tf_op jit(solution)/shard_map/all_to_all | solution.py:79
  240.2 0.2 fusion.27
  240.4 0.2 fusion.26
  240.6 1.1 stack.105
  241.7 6.5 %all-to-all-start.2 = ((bf16[16,2,32,512]{3,2,1,0:T(8,128)(2,1)}), bf16[16,2,32,512]{3,2,1,0:T(8,128)(2,1)S(1)}, u32[]{:S(2)}, u32[]{:S(2)}) async-start(bf16[16,2,32,512]{3,2,1,0:T(8,128)(2,1)} %stack.105), calls=%async_computation.2 | async-start | bytes 2097152 | tf_op jit(solution)/shard_map/all_to_all | solution.py:79
  248.3 11.8 %collective-permute-start.6 = (bf16[2,32,512]{2,1,0:T(8,128)(2,1)S(1)}, bf16[2,32,512]{2,1,0:T(8,128)(2,1)S(1)}, u32[]{:S(2)}, u32[]{:S(2)}) collective-permute-start(bf16[2,32,512]{2,1,0:T(8,128)(2,1)S(1)} %pad_maximum_fusion.4), channel_id=1, source_target_pairs={{0,448},{16,464},{32,480},{48,496},{64,0},{80,16},{96,32},{112,48}... | collective-permute-start | bytes 196616 | tf_op jit(solution)/shard_map/ppermute | solution.py:21
  260.1 3.3 all-to-all-done.2
  263.9 0.2 fusion.25
  264.4 1.1 stack.109
  265.5 6.9 %all-to-all-start.3 = ((bf16[16,2,32,512]{3,2,1,0:T(8,128)(2,1)}), bf16[16,2,32,512]{3,2,1,0:T(8,128)(2,1)S(1)}, u32[]{:S(2)}, u32[]{:S(2)}) async-start(bf16[16,2,32,512]{3,2,1,0:T(8,128)(2,1)} %stack.109), calls=%async_computation.3 | async-start | bytes 2097152 | tf_op jit(solution)/shard_map/all_to_all | solution.py:79
  272.4 12.3 %collective-permute-start.7 = (bf16[2,32,512]{2,1,0:T(8,128)(2,1)S(1)}, bf16[2,32,512]{2,1,0:T(8,128)(2,1)S(1)}, u32[]{:S(2)}, u32[]{:S(2)}) collective-permute-start(bf16[2,32,512]{2,1,0:T(8,128)(2,1)S(1)} %pad_maximum_fusion.5), channel_id=1, source_target_pairs={{0,384},{16,400},{32,416},{48,432},{64,448},{80,464},{96,480},{112... | collective-permute-start | bytes 196616 | tf_op jit(solution)/shard_map/ppermute | solution.py:21
  284.8 2.8 all-to-all-done.3
  287.6 3.0 collective-permute-done.7
  291.5 1.1 stack.113
  292.6 7.3 %all-to-all-start.4 = ((bf16[16,2,32,512]{3,2,1,0:T(8,128)(2,1)}), bf16[16,2,32,512]{3,2,1,0:T(8,128)(2,1)S(1)}, u32[]{:S(2)}, u32[]{:S(2)}) async-start(bf16[16,2,32,512]{3,2,1,0:T(8,128)(2,1)} %stack.113), calls=%async_computation.4 | async-start | bytes 2097152 | tf_op jit(solution)/shard_map/all_to_all | solution.py:79
  299.9 11.7 %collective-permute-start.8 = (bf16[2,32,512]{2,1,0:T(8,128)(2,1)S(1)}, bf16[2,32,512]{2,1,0:T(8,128)(2,1)S(1)}, u32[]{:S(2)}, u32[]{:S(2)}) collective-permute-start(bf16[2,32,512]{2,1,0:T(8,128)(2,1)S(1)} %pad_maximum_fusion.6), channel_id=1, source_target_pairs={{0,256},{16,272},{32,288},{48,304},{64,320},{80,336},{96,352},{112... | collective-permute-start | bytes 196616 | tf_op jit(solution)/shard_map/ppermute | solution.py:21
  311.5 3.4 all-to-all-done.4
  316.1 0.2 reshape.126
  316.3 29.2 %all_to_all.40 = bf16[32,2,512]{2,1,0:T(2,128)(2,1)S(1)} all-to-all(bf16[32,2,512]{2,1,0:T(2,128)(2,1)S(1)} %reshape.126), channel_id=1, replica_groups=mesh['cuts'=32,'blk'=16] {'cuts'}, dimensions={0} | all-to-all | bytes 131072 | tf_op jit(solution)/shard_map/all_to_all | solution.py:90
  345.7 0.4 copy.13
  346.1 0.2 fusion.38
  346.3 0.3 fusion.39
  346.6 0.3 convolution_add_fusion.4
  347.0 0.3 convolution_subtract_fusion.4
  347.5 1.3 copy.18
  (37 shorter events, 4.4 us)
Async XLA Ops:
  0.0 4.8 %collective-permute-start = (bf16[2,512,512]{2,1,0:T(8,128)(2,1)}, bf16[2,512,512]{2,1,0:T(8,128)(2,1)S(1)}, u32[]{:S(2)}, u32[]{:S(2)}) collective-permute-start(bf16[2,512,512]{2,1,0:T(8,128)(2,1)} %bitcast.227), channel_id=1, source_target_pairs={{0,1},{1,0},{2,3},{3,2},{4,5},{5,4},{6,7},{7,6},{8,9},{9,8},{10,11... | collective-permute-start | bytes 3145736 | tf_op jit(solution)/shard_map/ppermute | solution.py:16
  9.4 49.9 %collective-permute-start.1 = (f32[2,512,512]{2,1,0:T(8,128)}, f32[2,512,512]{2,1,0:T(8,128)}, u32[]{:S(2)}, u32[]{:S(2)}) collective-permute-start(f32[2,512,512]{2,1,0:T(8,128)} %pad_maximum_fusion), channel_id=1, source_target_pairs={{0,2},{2,0},{1,3},{3,1},{4,6},{6,4},{5,7},{7,5},{8,10},{10,8},{9,1... | collective-permute-start | bytes 6291464 | tf_op jit(solution)/shard_map/ppermute | solution.py:16
  70.5 50.5 %collective-permute-start.2 = (f32[2,512,512]{2,1,0:T(8,128)}, f32[2,512,512]{2,1,0:T(8,128)}, u32[]{:S(2)}, u32[]{:S(2)}) collective-permute-start(f32[2,512,512]{2,1,0:T(8,128)} %pad_maximum_fusion.1), channel_id=1, source_target_pairs={{0,4},{4,0},{1,5},{5,1},{2,6},{6,2},{3,7},{7,3},{8,12},{12,8},{9,1... | collective-permute-start | bytes 6291464 | tf_op jit(solution)/shard_map/ppermute | solution.py:16
  132.3 49.6 %collective-permute-start.3 = (f32[2,512,512]{2,1,0:T(8,128)}, f32[2,512,512]{2,1,0:T(8,128)}, u32[]{:S(2)}, u32[]{:S(2)}) collective-permute-start(f32[2,512,512]{2,1,0:T(8,128)} %pad_maximum_fusion.2), channel_id=1, source_target_pairs={{0,8},{8,0},{1,9},{9,1},{2,10},{10,2},{3,11},{11,3},{4,12},{12,4},... | collective-permute-start | bytes 6291464 | tf_op jit(solution)/shard_map/ppermute | solution.py:16
  192.9 23.0 %all-to-all-start = ((bf16[16,2,32,512]{3,2,1,0:T(8,128)(2,1)}), bf16[16,2,32,512]{3,2,1,0:T(8,128)(2,1)S(1)}, u32[]{:S(2)}, u32[]{:S(2)}) async-start(bf16[16,2,32,512]{3,2,1,0:T(8,128)(2,1)} %stack.97), calls=%async_computation | async-start | bytes 2097152 | tf_op jit(solution)/shard_map/all_to_all | solution.py:79
  200.4 15.7 %collective-permute-start.4 = (bf16[2,32,512]{2,1,0:T(8,128)(2,1)S(1)}, bf16[2,32,512]{2,1,0:T(8,128)(2,1)S(1)}, u32[]{:S(2)}, u32[]{:S(2)}) collective-permute-start(bf16[2,32,512]{2,1,0:T(8,128)(2,1)S(1)} %fusion.40), channel_id=1, source_target_pairs={{0,496},{16,0},{32,16},{48,32},{64,48},{80,64},{96,80},{112,96},{1... | collective-permute-start | bytes 196616 | tf_op jit(solution)/shard_map/ppermute | solution.py:21
  218.0 21.6 %all-to-all-start.1 = ((bf16[16,2,32,512]{3,2,1,0:T(8,128)(2,1)}), bf16[16,2,32,512]{3,2,1,0:T(8,128)(2,1)S(1)}, u32[]{:S(2)}, u32[]{:S(2)}) async-start(bf16[16,2,32,512]{3,2,1,0:T(8,128)(2,1)} %stack.101), calls=%async_computation.1 | async-start | bytes 2097152 | tf_op jit(solution)/shard_map/all_to_all | solution.py:79
  224.5 15.3 %collective-permute-start.5 = (bf16[2,32,512]{2,1,0:T(8,128)(2,1)S(1)}, bf16[2,32,512]{2,1,0:T(8,128)(2,1)S(1)}, u32[]{:S(2)}, u32[]{:S(2)}) collective-permute-start(bf16[2,32,512]{2,1,0:T(8,128)(2,1)S(1)} %pad_maximum_fusion.3), channel_id=1, source_target_pairs={{0,480},{16,496},{32,0},{48,16},{64,32},{80,48},{96,64},{112,80},{... | collective-permute-start | bytes 196616 | tf_op jit(solution)/shard_map/ppermute | solution.py:21
  241.7 21.7 %all-to-all-start.2 = ((bf16[16,2,32,512]{3,2,1,0:T(8,128)(2,1)}), bf16[16,2,32,512]{3,2,1,0:T(8,128)(2,1)S(1)}, u32[]{:S(2)}, u32[]{:S(2)}) async-start(bf16[16,2,32,512]{3,2,1,0:T(8,128)(2,1)} %stack.105), calls=%async_computation.2 | async-start | bytes 2097152 | tf_op jit(solution)/shard_map/all_to_all | solution.py:79
  248.3 15.3 %collective-permute-start.6 = (bf16[2,32,512]{2,1,0:T(8,128)(2,1)S(1)}, bf16[2,32,512]{2,1,0:T(8,128)(2,1)S(1)}, u32[]{:S(2)}, u32[]{:S(2)}) collective-permute-start(bf16[2,32,512]{2,1,0:T(8,128)(2,1)S(1)} %pad_maximum_fusion.4), channel_id=1, source_target_pairs={{0,448},{16,464},{32,480},{48,496},{64,0},{80,16},{96,32},{112,48}... | collective-permute-start | bytes 196616 | tf_op jit(solution)/shard_map/ppermute | solution.py:21
  265.5 22.0 %all-to-all-start.3 = ((bf16[16,2,32,512]{3,2,1,0:T(8,128)(2,1)}), bf16[16,2,32,512]{3,2,1,0:T(8,128)(2,1)S(1)}, u32[]{:S(2)}, u32[]{:S(2)}) async-start(bf16[16,2,32,512]{3,2,1,0:T(8,128)(2,1)} %stack.109), calls=%async_computation.3 | async-start | bytes 2097152 | tf_op jit(solution)/shard_map/all_to_all | solution.py:79
  272.4 18.2 %collective-permute-start.7 = (bf16[2,32,512]{2,1,0:T(8,128)(2,1)S(1)}, bf16[2,32,512]{2,1,0:T(8,128)(2,1)S(1)}, u32[]{:S(2)}, u32[]{:S(2)}) collective-permute-start(bf16[2,32,512]{2,1,0:T(8,128)(2,1)S(1)} %pad_maximum_fusion.5), channel_id=1, source_target_pairs={{0,384},{16,400},{32,416},{48,432},{64,448},{80,464},{96,480},{112... | collective-permute-start | bytes 196616 | tf_op jit(solution)/shard_map/ppermute | solution.py:21
  292.6 22.4 %all-to-all-start.4 = ((bf16[16,2,32,512]{3,2,1,0:T(8,128)(2,1)}), bf16[16,2,32,512]{3,2,1,0:T(8,128)(2,1)S(1)}, u32[]{:S(2)}, u32[]{:S(2)}) async-start(bf16[16,2,32,512]{3,2,1,0:T(8,128)(2,1)} %stack.113), calls=%async_computation.4 | async-start | bytes 2097152 | tf_op jit(solution)/shard_map/all_to_all | solution.py:79
  299.9 15.2 %collective-permute-start.8 = (bf16[2,32,512]{2,1,0:T(8,128)(2,1)S(1)}, bf16[2,32,512]{2,1,0:T(8,128)(2,1)S(1)}, u32[]{:S(2)}, u32[]{:S(2)}) collective-permute-start(bf16[2,32,512]{2,1,0:T(8,128)(2,1)S(1)} %pad_maximum_fusion.6), channel_id=1, source_target_pairs={{0,256},{16,272},{32,288},{48,304},{64,320},{80,336},{96,352},{112... | collective-permute-start | bytes 196616 | tf_op jit(solution)/shard_map/ppermute | solution.py:21
